TPU v7x, 512 devices: a whole 4x4x16 slice. The times are simulated.
512 devices in a mesh: face: 8 (over x, y_lo), tile: 64 (over z, y_hi, core).
Axes of the slice: x: 4, y: 4 (y_hi: 2, y_lo: 2; y = y_hi * 2 + y_lo), z: 16, core: 2. Of those that a mesh axis runs over, the one named last changes fastest.
Arguments:
- maps: bfloat16 [4, 4, 128, 8192], P(None, None, 'face', 'tile'), may hold values from -8 to 8
- params: float32 [4, 2], replicated, may hold values from 0 to 1
- labels: int32 [4], replicated, may hold values 0 or 1
- edge_flip: int32 [8, 64], replicated, may hold values from 0 to 1
- fine_weight: float32 [3, 4, 16], replicated, may hold values from -1.75 to 1.75
- coarse_weight: float32 [3, 16, 32], replicated, may hold values from -0.875 to 0.875
- feature_weight: float32 [32, 128], replicated, may hold values from -2 to 2
- param_weight: float32 [2, 128], replicated, may hold values from -4 to 4
- out_weight: float32 [128], replicated, may hold values from -1 to 1
Outputs:
- logits: float32 [4], replicated
- saliency: float32 [4, 4, 128, 8192], P(None, None, 'face', 'tile')
- grad_fine: float32 [3, 4, 16], replicated
- grad_coarse: float32 [3, 16, 32], replicated
All inputs are finite; a program needn't handle non-finite values.
Results may differ from a plain program's by a relative error of at most 0.0003.
Values sent between devices are 32-bit elements; how exact they have to be, the bound alone decides.
No kernel may reach another device: no remote copies, remote signals or barrier semaphores. Data moves between devices by JAX's collectives and lax.ppermute only.
A program may use at most 64 MiB of HBM per device.

v0:
```python
import jax
import jax.numpy as jnp
from jax import lax
from jax.sharding import PartitionSpec as P

exact = lax.Precision.HIGHEST


def with_halo(block, sides, width):
    for axis, dim in sides:
        count = lax.axis_size(axis)
        forward = [(i, i + 1) for i in range(count - 1)]
        forward.append((count - 1, 0))
        backward = [(target, source) for source, target in forward]
        low = lax.ppermute(
            lax.slice_in_dim(block, block.shape[dim] - width, None, axis=dim), axis, forward
        )
        high = lax.ppermute(lax.slice_in_dim(block, 0, width, axis=dim), axis, backward)
        block = jnp.concatenate([low, block, high], axis=dim)
    return block


def turn_blocks(edge_row, width):
    lead = edge_row.shape[:-1]
    return edge_row.reshape(lead + (-1, width))[..., ::-1].reshape(edge_row.shape)


def face_flags(edge_flip):
    position = lax.axis_index("face")
    faces = edge_flip.shape[0]
    return (edge_flip[position] == 1, edge_flip[(position + 1) % faces] == 1)


def tile_flags(flags):
    tiles = flags[0].shape[0]
    spot = lax.axis_index("tile") % tiles
    return (flags[0][spot], flags[1][spot])


def stencil(padded, flags, width):
    top_flag, bottom_flag = tile_flags(flags)
    left = padded[..., 1:-1, :-2]
    right = padded[..., 1:-1, 2:]
    upper = padded[..., :-2, 1:-1]
    lower = padded[..., 2:, 1:-1]
    top_row = upper[..., 0, :]
    upper = upper.at[..., 0, :].set(jnp.where(top_flag, turn_blocks(top_row, width), top_row))
    bottom_row = lower[..., -1, :]
    lower = lower.at[..., -1, :].set(
        jnp.where(bottom_flag, turn_blocks(bottom_row, width), bottom_row)
    )
    return -0.25 * (upper + lower + left + right)


def fine_apply(field, flags):
    padded = with_halo(field, (("face", 2), ("tile", 3)), 1)
    return stencil(padded, flags, field.shape[-1])


def coarse_apply(field, flags):
    padded = with_halo(field, (("face", 2), ("tile", 3)), 1)
    return stencil(padded, flags, field.shape[-1])


def coarse_terms(field, flags):
    first = coarse_apply(field, flags)
    second = 2.0 * coarse_apply(first, flags) - field
    return (first, second)


def coarse_adjoint(parts, flags):
    inner = coarse_apply(parts[2], flags)
    outer = coarse_apply(parts[1] + 2.0 * inner, flags)
    return parts[0] - parts[2] + outer


def on_device(
    maps,
    params,
    labels,
    edge_flip,
    fine_weight,
    coarse_weight,
    feature_weight,
    param_weight,
    out_weight,
):
    flags = face_flags(edge_flip)
    field0 = maps.astype(jnp.float32)
    first0 = fine_apply(field0, flags)
    second0 = 2.0 * fine_apply(first0, flags) - field0
    terms0 = jnp.stack([field0, first0, second0])
    pre0 = jnp.einsum("kio,kbirc->borc", fine_weight, terms0, precision=exact)
    act0 = jax.nn.softplus(pre0)
    nmaps, nchan, nrows, ncols = act0.shape
    field1 = act0.reshape(nmaps, nchan, nrows // 2, 2, ncols // 2, 2).mean(axis=(3, 5))
    first1, second1 = coarse_terms(field1, flags)
    terms1 = jnp.stack([field1, first1, second1])
    pre1 = jnp.einsum("kio,kbirc->borc", coarse_weight, terms1, precision=exact)
    act1 = jax.nn.softplus(pre1)
    pooled_count = nrows // 2 * lax.axis_size("face") * (ncols // 2) * lax.axis_size("tile")
    features = lax.psum(act1.sum(axis=(2, 3)), ("face", "tile")) / pooled_count
    hidden = jnp.tanh(
        jnp.dot(features, feature_weight, precision=exact)
        + jnp.dot(params, param_weight, precision=exact)
    )
    logits = jnp.dot(hidden, out_weight, precision=exact)
    dlogit = jax.nn.sigmoid(logits) - labels.astype(jnp.float32)
    dhidden = dlogit[:, None] * out_weight[None, :] * (1.0 - hidden * hidden)
    dfeatures = jnp.dot(dhidden, feature_weight.T, precision=exact)
    dpre1 = (dfeatures / pooled_count)[:, :, None, None] * jax.nn.sigmoid(pre1)
    grad_c = jnp.einsum("kbirc,borc->kio", terms1, dpre1, precision=exact)
    parts1 = jnp.einsum("kio,borc->kbirc", coarse_weight, dpre1, precision=exact)
    dfield1 = coarse_adjoint(parts1, flags)
    spread = jnp.broadcast_to(
        dfield1[:, :, :, None, :, None], (nmaps, nchan, nrows // 2, 2, ncols // 2, 2)
    ).reshape(pre0.shape)
    dpre0 = 0.25 * spread * jax.nn.sigmoid(pre0)
    grad_f = jnp.einsum("kbirc,borc->kio", terms0, dpre0, precision=exact)
    parts0 = jnp.einsum("kio,borc->kbirc", fine_weight, dpre0, precision=exact)
    inner0 = fine_apply(parts0[2], flags)
    outer0 = fine_apply(parts0[1] + 2.0 * inner0, flags)
    pixel_count = nrows * lax.axis_size("face") * ncols * lax.axis_size("tile")
    saliency = (parts0[0] - parts0[2] + outer0) * pixel_count
    grad_f, grad_c = lax.psum((grad_f, grad_c), ("face", "tile"))
    return (logits, saliency, grad_f, grad_c)


def solution(mesh):
    in_specs = (P(None, None, "face", "tile"), P(), P(), P(), P(), P(), P(), P(), P())
    out_specs = (P(), P(None, None, "face", "tile"), P(), P())
    return jax.shard_map(
        on_device, mesh=mesh, in_specs=in_specs, out_specs=out_specs, check_vma=False
    )
```

profile of v0, /device:TPU:1, one launch (start us, length us, event | category | flops | bytes accessed | tf_op | source)
XLA Modules:
  0.0 429.5 jit_solution(592526183360856192)
XLA Ops:
  0.7 0.9 fusion.42
  1.6 4.0 collective-permute-start
  5.6 4.1 collective-permute-start.1
  9.8 0.8 fusion.58
  12.0 6.0 %collective-permute-start.2 = (f32[4,4,18,1]{3,1,2,0:T(4,128)S(1)}, f32[4,4,18,1]{3,1,2,0:T(4,128)S(1)}, u32[]{:S(2)}, u32[]{:S(2)}) collective-permute-start(f32[4,4,18,1]{3,1,2,0:T(4,128)S(1)} %get-tuple-element.242), channel_id=1, source_target_pairs={{0,1},{1,2},{2,3},{3,4},{4,5},{5,6},{6,7},{7,8},{8,9},{9,10},{10,1... | collective-permute-start | bytes 3464 | tf_op jit(solution)/shard_map/ppermute | solution.py:15
  18.1 4.5 %collective-permute-start.3 = (f32[4,4,18,1]{3,1,2,0:T(4,128)S(1)}, f32[4,4,18,1]{3,1,2,0:T(4,128)S(1)}, u32[]{:S(2)}, u32[]{:S(2)}) collective-permute-start(f32[4,4,18,1]{3,1,2,0:T(4,128)S(1)} %get-tuple-element.243), channel_id=1, source_target_pairs={{1,0},{2,1},{3,2},{4,3},{5,4},{6,5},{7,6},{8,7},{9,8},{10,9},{11,1... | collective-permute-start | bytes 3464 | tf_op jit(solution)/shard_map/ppermute | solution.py:18
  22.8 1.3 select_dynamic-update-slice_fusion.14
  24.2 1.9 collective-permute-done.3
  26.3 2.6 collective-permute-start.4
  28.9 4.8 %collective-permute-start.5 = (f32[4,4,1,128]{3,1,2,0:T(4,128)S(1)}, f32[4,4,1,128]{3,1,2,0:T(4,128)S(1)}, u32[]{:S(2)}, u32[]{:S(2)}) collective-permute-start(f32[4,4,1,128]{3,1,2,0:T(4,128)S(1)} %get-tuple-element.255), channel_id=1, source_target_pairs={{64,0},{128,64},{192,128},{256,192},{320,256},{384,320},{448,384},... | collective-permute-start | bytes 24584 | tf_op jit(solution)/shard_map/ppermute | solution.py:18
  33.7 0.8 collective-permute-done.5
  34.7 2.9 collective-permute-start.6
  37.6 6.9 %collective-permute-start.7 = (f32[4,4,18,1]{3,1,2,0:T(4,128)S(1)}, f32[4,4,18,1]{3,1,2,0:T(4,128)S(1)}, u32[]{:S(2)}, u32[]{:S(2)}) collective-permute-start(f32[4,4,18,1]{3,1,2,0:T(4,128)S(1)} %get-tuple-element.241), channel_id=1, source_target_pairs={{1,0},{2,1},{3,2},{4,3},{5,4},{6,5},{7,6},{8,7},{9,8},{10,9},{11,1... | collective-permute-start | bytes 3464 | tf_op jit(solution)/shard_map/ppermute | solution.py:18
  44.7 0.7 select_dynamic-update-slice_fusion.12
  46.1 1.1 fusion.37
  47.2 1.7 compare_select_fusion.1
  49.0 2.6 copy.39
  51.6 5.6 %reduce_sum.18 = f32[4,16,8,64]{1,3,2,0:T(8,128)S(1)} reduce(f32[4,16,8,2,64,2]{1,5,4,3,2,0:T(2,128)} %bitcast.121, f32[]{:T(128)} %constant.422.clone.1), dimensions={3,5}, to_apply=%region_0.1 | reduce | flops 98304 | bytes 655364 | tf_op jit(solution)/shard_map/reduce_sum | solution.py:96
  57.6 2.5 collective-permute-start.8
  60.1 5.4 %collective-permute-start.9 = (f32[4,16,1,64]{3,1,2,0:T(8,128)S(1)}, f32[4,16,1,64]{3,1,2,0:T(8,128)S(1)}, u32[]{:S(2)}, u32[]{:S(2)}) collective-permute-start(f32[4,16,1,64]{3,1,2,0:T(8,128)S(1)} %get-tuple-element.235), channel_id=1, source_target_pairs={{64,0},{128,64},{192,128},{256,192},{320,256},{384,320},{448,384},... | collective-permute-start | bytes 49160 | tf_op jit(solution)/shard_map/ppermute | solution.py:18
  65.6 1.0 collective-permute-done.9
  66.8 2.1 collective-permute-start.10
  68.8 9.0 %collective-permute-start.11 = (f32[4,16,10,1]{3,1,2,0:T(8,128)S(1)}, f32[4,16,10,1]{3,1,2,0:T(8,128)S(1)}, u32[]{:S(2)}, u32[]{:S(2)}) collective-permute-start(f32[4,16,10,1]{3,1,2,0:T(8,128)S(1)} %get-tuple-element.217), channel_id=1, source_target_pairs={{1,0},{2,1},{3,2},{4,3},{5,4},{6,5},{7,6},{8,7},{9,8},{10,9},{11,1... | collective-permute-start | bytes 7688 | tf_op jit(solution)/shard_map/ppermute | solution.py:18
  79.8 1.9 collective-permute-start.12
  81.7 6.2 %collective-permute-start.13 = (f32[4,16,1,64]{3,1,2,0:T(8,128)S(1)}, f32[4,16,1,64]{3,1,2,0:T(8,128)S(1)}, u32[]{:S(2)}, u32[]{:S(2)}) collective-permute-start(f32[4,16,1,64]{3,1,2,0:T(8,128)S(1)} %get-tuple-element.231), channel_id=1, source_target_pairs={{64,0},{128,64},{192,128},{256,192},{320,256},{384,320},{448,384},... | collective-permute-start | bytes 49160 | tf_op jit(solution)/shard_map/ppermute | solution.py:18
  87.9 1.0 collective-permute-done.13
  89.1 2.0 collective-permute-start.14
  91.0 11.0 %collective-permute-start.15 = (f32[4,16,10,1]{3,1,2,0:T(8,128)S(1)}, f32[4,16,10,1]{3,1,2,0:T(8,128)S(1)}, u32[]{:S(2)}, u32[]{:S(2)}) collective-permute-start(f32[4,16,10,1]{3,1,2,0:T(8,128)S(1)} %get-tuple-element.215), channel_id=1, source_target_pairs={{1,0},{2,1},{3,2},{4,3},{5,4},{6,5},{7,6},{8,7},{9,8},{10,9},{11,1... | collective-permute-start | bytes 7688 | tf_op jit(solution)/shard_map/ppermute | solution.py:18
  104.7 1.0 fusion.1
  105.7 115.2 %psum.21 = f32[4,32]{1,0:T(4,128)S(1)} all-reduce(f32[4,32]{1,0:T(4,128)S(1)} %get-tuple-element.266), channel_id=1, replica_groups=mesh['face'=8,'tile'=64] {'face','tile'}, use_global_device_ids=true, to_apply=%region_2.3 | all-reduce | flops 128 | bytes 1024 | tf_op jit(solution)/shard_map/psum | solution.py:102
  222.1 0.9 convolution_bitcast_fusion
  223.1 1.9 collective-permute-start.16
  225.0 5.5 %collective-permute-start.17 = (f32[4,16,1,64]{3,1,2,0:T(8,128)S(1)}, f32[4,16,1,64]{3,1,2,0:T(8,128)S(1)}, u32[]{:S(2)}, u32[]{:S(2)}) collective-permute-start(f32[4,16,1,64]{3,1,2,0:T(8,128)S(1)} %get-tuple-element.225), channel_id=1, source_target_pairs={{64,0},{128,64},{192,128},{256,192},{320,256},{384,320},{448,384},... | collective-permute-start | bytes 49160 | tf_op jit(solution)/shard_map/ppermute | solution.py:18
  230.5 1.0 collective-permute-done.17
  231.5 0.9 fusion.70
  232.4 4.7 %collective-permute-start.18 = (f32[4,16,10,1]{3,1,2,0:T(8,128)}, f32[4,16,10,1]{3,1,2,0:T(8,128)S(1)}, u32[]{:S(2)}, u32[]{:S(2)}) collective-permute-start(f32[4,16,10,1]{3,1,2,0:T(8,128)} %get-tuple-element.212), channel_id=1, source_target_pairs={{0,1},{1,2},{2,3},{3,4},{4,5},{5,6},{6,7},{7,8},{8,9},{9,10},{10,1... | collective-permute-start | bytes 7688 | tf_op jit(solution)/shard_map/ppermute | solution.py:15
  237.1 2.1 collective-permute-start.19
  241.4 8.2 %collective-permute-done.19 = f32[4,16,10,1]{3,1,2,0:T(8,128)S(1)} collective-permute-done((f32[4,16,10,1]{3,1,2,0:T(8,128)S(1)}, f32[4,16,10,1]{3,1,2,0:T(8,128)S(1)}, u32[]{:S(2)}, u32[]{:S(2)}) %collective-permute-start.19) | collective-permute-done | bytes 2592 | tf_op jit(solution)/shard_map/ppermute | solution.py:18
  249.9 1.9 collective-permute-start.20
  251.8 6.1 %collective-permute-start.21 = (f32[4,16,1,64]{3,1,2,0:T(8,128)S(1)}, f32[4,16,1,64]{3,1,2,0:T(8,128)S(1)}, u32[]{:S(2)}, u32[]{:S(2)}) collective-permute-start(f32[4,16,1,64]{3,1,2,0:T(8,128)S(1)} %get-tuple-element.221), channel_id=1, source_target_pairs={{64,0},{128,64},{192,128},{256,192},{320,256},{384,320},{448,384},... | collective-permute-start | bytes 49160 | tf_op jit(solution)/shard_map/ppermute | solution.py:18
  257.9 1.0 collective-permute-done.21
  258.9 0.9 fusion.69
  259.8 3.3 collective-permute-start.22
  263.1 1.9 collective-permute-start.23
  266.6 4.3 %collective-permute-done.22 = f32[4,16,10,1]{3,1,2,0:T(8,128)S(1)} collective-permute-done((f32[4,16,10,1]{3,1,2,0:T(8,128)}, f32[4,16,10,1]{3,1,2,0:T(8,128)S(1)}, u32[]{:S(2)}, u32[]{:S(2)}) %collective-permute-start.22) | collective-permute-done | bytes 2592 | tf_op jit(solution)/shard_map/ppermute | solution.py:15
  271.0 4.1 collective-permute-done.23
  275.7 4.0 broadcast_in_dim.2
  279.7 2.8 copy.45
  282.6 0.9 convolution_bitcast_fusion.3
  283.5 1.9 collective-permute-start.24
  285.4 5.5 %collective-permute-start.25 = (f32[4,4,1,128]{3,1,2,0:T(4,128)S(1)}, f32[4,4,1,128]{3,1,2,0:T(4,128)S(1)}, u32[]{:S(2)}, u32[]{:S(2)}) collective-permute-start(f32[4,4,1,128]{3,1,2,0:T(4,128)S(1)} %get-tuple-element.251), channel_id=1, source_target_pairs={{64,0},{128,64},{192,128},{256,192},{320,256},{384,320},{448,384},... | collective-permute-start | bytes 24584 | tf_op jit(solution)/shard_map/ppermute | solution.py:18
  290.9 0.9 convolution_bitcast_fusion.4
  292.1 3.0 collective-permute-start.26
  295.1 1.9 collective-permute-start.27
  297.2 0.7 select_dynamic-update-slice_fusion.10
  298.7 4.3 %collective-permute-done.27 = f32[4,4,18,1]{3,1,2,0:T(4,128)S(1)} collective-permute-done((f32[4,4,18,1]{3,1,2,0:T(4,128)S(1)}, f32[4,4,18,1]{3,1,2,0:T(4,128)S(1)}, u32[]{:S(2)}, u32[]{:S(2)}) %collective-permute-start.27) | collective-permute-done | bytes 1184 | tf_op jit(solution)/shard_map/ppermute | solution.py:18
  303.3 1.9 collective-permute-start.28
  305.2 5.7 %collective-permute-start.29 = (f32[4,4,1,128]{3,1,2,0:T(4,128)S(1)}, f32[4,4,1,128]{3,1,2,0:T(4,128)S(1)}, u32[]{:S(2)}, u32[]{:S(2)}) collective-permute-start(f32[4,4,1,128]{3,1,2,0:T(4,128)S(1)} %get-tuple-element.247), channel_id=1, source_target_pairs={{64,0},{128,64},{192,128},{256,192},{320,256},{384,320},{448,384},... | collective-permute-start | bytes 24584 | tf_op jit(solution)/shard_map/ppermute | solution.py:18
  311.0 1.7 convolution_bitcast_fusion.5
  312.6 103.5 %all-reduce = (f32[3,4,16]{2,1,0:T(4,128)}, f32[3,16,32]{2,1,0:T(8,128)}) all-reduce(f32[3,4,16]{2,1,0:T(4,128)S(1)} %convolution_bitcast_fusion.5, f32[3,16,32]{2,1,0:T(8,128)S(1)} %convolution_bitcast_fusion.4), channel_id=1, replica_groups=mesh['face'=8,'tile'=64] {'face','tile'}, use_global_device_ids=true, to_apply=%region_3.4 | all-reduce | flops 1728 | bytes 13824 | tf_op jit(solution)/shard_map/psum | solution.py:125
  416.4 4.2 collective-permute-start.30
  420.6 1.9 collective-permute-start.31
  422.7 0.7 select_dynamic-update-slice_fusion.8
  424.1 4.4 %collective-permute-done.31 = f32[4,4,18,1]{3,1,2,0:T(4,128)S(1)} collective-permute-done((f32[4,4,18,1]{3,1,2,0:T(4,128)S(1)}, f32[4,4,18,1]{3,1,2,0:T(4,128)S(1)}, u32[]{:S(2)}, u32[]{:S(2)}) %collective-permute-start.31) | collective-permute-done | bytes 1184 | tf_op jit(solution)/shard_map/ppermute | solution.py:18
  (129 shorter events, 17.6 us)
Async XLA Ops:
  0.6 104.0 %copy-start = (f32[3,16,32]{2,1,0:T(8,128)S(1)}, f32[3,16,32]{2,1,0:T(8,128)}, u32[]{:S(2)}) copy-start(f32[3,16,32]{2,1,0:T(8,128)} %param.46) | copy-start | bytes 18436
  0.6 46.6 %copy-start.12 = (f32[3,4,16]{2,1,0:T(4,128)S(1)}, f32[3,4,16]{2,1,0:T(4,128)}, u32[]{:S(2)}) copy-start(f32[3,4,16]{2,1,0:T(4,128)} %param.45) | copy-start | bytes 2308
  1.6 50.0 %copy-start.7 = (f32[1,4,4,16,128]{4,2,0,3,1:T(4,128)}, f32[1,4,4,16,128]{4,2,0,3,1:T(4,128)S(1)}, u32[]{:S(2)}) copy-start(f32[1,4,4,16,128]{4,2,0,3,1:T(4,128)S(1)} %get-tuple-element.260) | copy-start | bytes 393220
  1.6 10.3 %collective-permute-start = (f32[4,4,1,128]{3,1,2,0:T(4,128)S(1)}, f32[4,4,1,128]{3,1,2,0:T(4,128)S(1)}, u32[]{:S(2)}, u32[]{:S(2)}) collective-permute-start(f32[4,4,1,128]{3,1,2,0:T(4,128)S(1)} %get-tuple-element.258), channel_id=1, source_target_pairs={{0,64},{64,128},{128,192},{192,256},{256,320},{320,384},{384,448},... | collective-permute-start | bytes 24584 | tf_op jit(solution)/shard_map/ppermute | solution.py:15
  5.6 6.2 %collective-permute-start.1 = (f32[4,4,1,128]{3,1,2,0:T(4,128)S(1)}, f32[4,4,1,128]{3,1,2,0:T(4,128)S(1)}, u32[]{:S(2)}, u32[]{:S(2)}) collective-permute-start(f32[4,4,1,128]{3,1,2,0:T(4,128)S(1)} %get-tuple-element.259), channel_id=1, source_target_pairs={{64,0},{128,64},{192,128},{256,192},{320,256},{384,320},{448,384},... | collective-permute-start | bytes 24584 | tf_op jit(solution)/shard_map/ppermute | solution.py:18
  12.0 12.1 %collective-permute-start.2 = (f32[4,4,18,1]{3,1,2,0:T(4,128)S(1)}, f32[4,4,18,1]{3,1,2,0:T(4,128)S(1)}, u32[]{:S(2)}, u32[]{:S(2)}) collective-permute-start(f32[4,4,18,1]{3,1,2,0:T(4,128)S(1)} %get-tuple-element.242), channel_id=1, source_target_pairs={{0,1},{1,2},{2,3},{3,4},{4,5},{5,6},{6,7},{7,8},{8,9},{9,10},{10,1... | collective-permute-start | bytes 3464 | tf_op jit(solution)/shard_map/ppermute | solution.py:15
  18.1 8.0 %collective-permute-start.3 = (f32[4,4,18,1]{3,1,2,0:T(4,128)S(1)}, f32[4,4,18,1]{3,1,2,0:T(4,128)S(1)}, u32[]{:S(2)}, u32[]{:S(2)}) collective-permute-start(f32[4,4,18,1]{3,1,2,0:T(4,128)S(1)} %get-tuple-element.243), channel_id=1, source_target_pairs={{1,0},{2,1},{3,2},{4,3},{5,4},{6,5},{7,6},{8,7},{9,8},{10,9},{11,1... | collective-permute-start | bytes 3464 | tf_op jit(solution)/shard_map/ppermute | solution.py:18
  26.3 7.4 %collective-permute-start.4 = (f32[4,4,1,128]{3,1,2,0:T(4,128)S(1)}, f32[4,4,1,128]{3,1,2,0:T(4,128)S(1)}, u32[]{:S(2)}, u32[]{:S(2)}) collective-permute-start(f32[4,4,1,128]{3,1,2,0:T(4,128)S(1)} %get-tuple-element.254), channel_id=1, source_target_pairs={{0,64},{64,128},{128,192},{192,256},{256,320},{320,384},{384,448},... | collective-permute-start | bytes 24584 | tf_op jit(solution)/shard_map/ppermute | solution.py:15
  28.9 5.6 %collective-permute-start.5 = (f32[4,4,1,128]{3,1,2,0:T(4,128)S(1)}, f32[4,4,1,128]{3,1,2,0:T(4,128)S(1)}, u32[]{:S(2)}, u32[]{:S(2)}) collective-permute-start(f32[4,4,1,128]{3,1,2,0:T(4,128)S(1)} %get-tuple-element.255), channel_id=1, source_target_pairs={{64,0},{128,64},{192,128},{256,192},{320,256},{384,320},{448,384},... | collective-permute-start | bytes 24584 | tf_op jit(solution)/shard_map/ppermute | solution.py:18
  34.7 11.4 %collective-permute-start.6 = (f32[4,4,18,1]{3,1,2,0:T(4,128)S(1)}, f32[4,4,18,1]{3,1,2,0:T(4,128)S(1)}, u32[]{:S(2)}, u32[]{:S(2)}) collective-permute-start(f32[4,4,18,1]{3,1,2,0:T(4,128)S(1)} %get-tuple-element.240), channel_id=1, source_target_pairs={{0,1},{1,2},{2,3},{3,4},{4,5},{5,6},{6,7},{7,8},{8,9},{9,10},{10,1... | collective-permute-start | bytes 3464 | tf_op jit(solution)/shard_map/ppermute | solution.py:15
  37.6 8.5 %collective-permute-start.7 = (f32[4,4,18,1]{3,1,2,0:T(4,128)S(1)}, f32[4,4,18,1]{3,1,2,0:T(4,128)S(1)}, u32[]{:S(2)}, u32[]{:S(2)}) collective-permute-start(f32[4,4,18,1]{3,1,2,0:T(4,128)S(1)} %get-tuple-element.241), channel_id=1, source_target_pairs={{1,0},{2,1},{3,2},{4,3},{5,4},{6,5},{7,6},{8,7},{9,8},{10,9},{11,1... | collective-permute-start | bytes 3464 | tf_op jit(solution)/shard_map/ppermute | solution.py:18
  47.2 4.4 %copy-start.5 = (f32[1,4,4,16,128]{4,2,0,3,1:T(4,128)}, f32[1,4,4,16,128]{4,2,0,3,1:T(4,128)S(1)}, u32[]{:S(2)}) copy-start(f32[1,4,4,16,128]{4,2,0,3,1:T(4,128)S(1)} %fusion.37) | copy-start | bytes 393220
  57.6 8.0 %collective-permute-start.8 = (f32[4,16,1,64]{3,1,2,0:T(8,128)S(1)}, f32[4,16,1,64]{3,1,2,0:T(8,128)S(1)}, u32[]{:S(2)}, u32[]{:S(2)}) collective-permute-start(f32[4,16,1,64]{3,1,2,0:T(8,128)S(1)} %get-tuple-element.234), channel_id=1, source_target_pairs={{0,64},{64,128},{128,192},{192,256},{256,320},{320,384},{384,448},... | collective-permute-start | bytes 49160 | tf_op jit(solution)/shard_map/ppermute | solution.py:15
  60.1 6.4 %collective-permute-start.9 = (f32[4,16,1,64]{3,1,2,0:T(8,128)S(1)}, f32[4,16,1,64]{3,1,2,0:T(8,128)S(1)}, u32[]{:S(2)}, u32[]{:S(2)}) collective-permute-start(f32[4,16,1,64]{3,1,2,0:T(8,128)S(1)} %get-tuple-element.235), channel_id=1, source_target_pairs={{64,0},{128,64},{192,128},{256,192},{320,256},{384,320},{448,384},... | collective-permute-start | bytes 49160 | tf_op jit(solution)/shard_map/ppermute | solution.py:18
  66.8 12.6 %collective-permute-start.10 = (f32[4,16,10,1]{3,1,2,0:T(8,128)S(1)}, f32[4,16,10,1]{3,1,2,0:T(8,128)S(1)}, u32[]{:S(2)}, u32[]{:S(2)}) collective-permute-start(f32[4,16,10,1]{3,1,2,0:T(8,128)S(1)} %get-tuple-element.216), channel_id=1, source_target_pairs={{0,1},{1,2},{2,3},{3,4},{4,5},{5,6},{6,7},{7,8},{8,9},{9,10},{10,1... | collective-permute-start | bytes 7688 | tf_op jit(solution)/shard_map/ppermute | solution.py:15
  68.8 10.6 %collective-permute-start.11 = (f32[4,16,10,1]{3,1,2,0:T(8,128)S(1)}, f32[4,16,10,1]{3,1,2,0:T(8,128)S(1)}, u32[]{:S(2)}, u32[]{:S(2)}) collective-permute-start(f32[4,16,10,1]{3,1,2,0:T(8,128)S(1)} %get-tuple-element.217), channel_id=1, source_target_pairs={{1,0},{2,1},{3,2},{4,3},{5,4},{6,5},{7,6},{8,7},{9,8},{10,9},{11,1... | collective-permute-start | bytes 7688 | tf_op jit(solution)/shard_map/ppermute | solution.py:18
  79.7 141.2 %copy-start.9 = (f32[32,128]{1,0:T(8,128)S(1)}, f32[32,128]{1,0:T(8,128)}, u32[]{:S(2)}) copy-start(f32[32,128]{1,0:T(8,128)} %param.47) | copy-start | bytes 49156
  79.7 141.3 %copy-start.10 = (f32[4,2]{0,1:T(2,128)S(1)}, f32[4,2]{0,1:T(2,128)}, u32[]{:S(2)}) copy-start(f32[4,2]{0,1:T(2,128)} %param.42) | copy-start | bytes 100
  79.7 141.3 %copy-start.11 = (f32[2,128]{1,0:T(2,128)S(1)}, f32[2,128]{1,0:T(2,128)}, u32[]{:S(2)}) copy-start(f32[2,128]{1,0:T(2,128)} %param.48) | copy-start | bytes 3076
  79.7 141.5 %copy-start.13 = (s32[4]{0:T(128)S(1)}, s32[4]{0:T(128)}, u32[]{:S(2)}) copy-start(s32[4]{0:T(128)} %param.43) | copy-start | bytes 52
  79.8 141.5 %copy-start.14 = (f32[128]{0:T(128)S(1)}, f32[128]{0:T(128)}, u32[]{:S(2)}) copy-start(f32[128]{0:T(128)} %param.49) | copy-start | bytes 1540
  79.8 8.1 %collective-permute-start.12 = (f32[4,16,1,64]{3,1,2,0:T(8,128)S(1)}, f32[4,16,1,64]{3,1,2,0:T(8,128)S(1)}, u32[]{:S(2)}, u32[]{:S(2)}) collective-permute-start(f32[4,16,1,64]{3,1,2,0:T(8,128)S(1)} %get-tuple-element.230), channel_id=1, source_target_pairs={{0,64},{64,128},{128,192},{192,256},{256,320},{320,384},{384,448},... | collective-permute-start | bytes 49160 | tf_op jit(solution)/shard_map/ppermute | solution.py:15
  81.7 7.2 %collective-permute-start.13 = (f32[4,16,1,64]{3,1,2,0:T(8,128)S(1)}, f32[4,16,1,64]{3,1,2,0:T(8,128)S(1)}, u32[]{:S(2)}, u32[]{:S(2)}) collective-permute-start(f32[4,16,1,64]{3,1,2,0:T(8,128)S(1)} %get-tuple-element.231), channel_id=1, source_target_pairs={{64,0},{128,64},{192,128},{256,192},{320,256},{384,320},{448,384},... | collective-permute-start | bytes 49160 | tf_op jit(solution)/shard_map/ppermute | solution.py:18
  89.1 14.6 %collective-permute-start.14 = (f32[4,16,10,1]{3,1,2,0:T(8,128)S(1)}, f32[4,16,10,1]{3,1,2,0:T(8,128)S(1)}, u32[]{:S(2)}, u32[]{:S(2)}) collective-permute-start(f32[4,16,10,1]{3,1,2,0:T(8,128)S(1)} %get-tuple-element.214), channel_id=1, source_target_pairs={{0,1},{1,2},{2,3},{3,4},{4,5},{5,6},{6,7},{7,8},{8,9},{9,10},{10,1... | collective-permute-start | bytes 7688 | tf_op jit(solution)/shard_map/ppermute | solution.py:15
  91.0 12.6 %collective-permute-start.15 = (f32[4,16,10,1]{3,1,2,0:T(8,128)S(1)}, f32[4,16,10,1]{3,1,2,0:T(8,128)S(1)}, u32[]{:S(2)}, u32[]{:S(2)}) collective-permute-start(f32[4,16,10,1]{3,1,2,0:T(8,128)S(1)} %get-tuple-element.215), channel_id=1, source_target_pairs={{1,0},{2,1},{3,2},{4,3},{5,4},{6,5},{7,6},{8,7},{9,8},{10,9},{11,1... | collective-permute-start | bytes 7688 | tf_op jit(solution)/shard_map/ppermute | solution.py:18
  104.0 0.7 copy-start.1
  104.0 1.7 copy-start.3
  223.1 7.4 %collective-permute-start.16 = (f32[4,16,1,64]{3,1,2,0:T(8,128)S(1)}, f32[4,16,1,64]{3,1,2,0:T(8,128)S(1)}, u32[]{:S(2)}, u32[]{:S(2)}) collective-permute-start(f32[4,16,1,64]{3,1,2,0:T(8,128)S(1)} %get-tuple-element.224), channel_id=1, source_target_pairs={{0,64},{64,128},{128,192},{192,256},{256,320},{320,384},{384,448},... | collective-permute-start | bytes 49160 | tf_op jit(solution)/shard_map/ppermute | solution.py:15
  225.0 6.5 %collective-permute-start.17 = (f32[4,16,1,64]{3,1,2,0:T(8,128)S(1)}, f32[4,16,1,64]{3,1,2,0:T(8,128)S(1)}, u32[]{:S(2)}, u32[]{:S(2)}) collective-permute-start(f32[4,16,1,64]{3,1,2,0:T(8,128)S(1)} %get-tuple-element.225), channel_id=1, source_target_pairs={{64,0},{128,64},{192,128},{256,192},{320,256},{384,320},{448,384},... | collective-permute-start | bytes 49160 | tf_op jit(solution)/shard_map/ppermute | solution.py:18
  232.4 9.0 %collective-permute-start.18 = (f32[4,16,10,1]{3,1,2,0:T(8,128)}, f32[4,16,10,1]{3,1,2,0:T(8,128)S(1)}, u32[]{:S(2)}, u32[]{:S(2)}) collective-permute-start(f32[4,16,10,1]{3,1,2,0:T(8,128)} %get-tuple-element.212), channel_id=1, source_target_pairs={{0,1},{1,2},{2,3},{3,4},{4,5},{5,6},{6,7},{7,8},{8,9},{9,10},{10,1... | collective-permute-start | bytes 7688 | tf_op jit(solution)/shard_map/ppermute | solution.py:15
  237.1 12.5 %collective-permute-start.19 = (f32[4,16,10,1]{3,1,2,0:T(8,128)S(1)}, f32[4,16,10,1]{3,1,2,0:T(8,128)S(1)}, u32[]{:S(2)}, u32[]{:S(2)}) collective-permute-start(f32[4,16,10,1]{3,1,2,0:T(8,128)S(1)} %get-tuple-element.213), channel_id=1, source_target_pairs={{1,0},{2,1},{3,2},{4,3},{5,4},{6,5},{7,6},{8,7},{9,8},{10,9},{11,1... | collective-permute-start | bytes 7688 | tf_op jit(solution)/shard_map/ppermute | solution.py:18
  249.9 8.0 %collective-permute-start.20 = (f32[4,16,1,64]{3,1,2,0:T(8,128)S(1)}, f32[4,16,1,64]{3,1,2,0:T(8,128)S(1)}, u32[]{:S(2)}, u32[]{:S(2)}) collective-permute-start(f32[4,16,1,64]{3,1,2,0:T(8,128)S(1)} %get-tuple-element.220), channel_id=1, source_target_pairs={{0,64},{64,128},{128,192},{192,256},{256,320},{320,384},{384,448},... | collective-permute-start | bytes 49160 | tf_op jit(solution)/shard_map/ppermute | solution.py:15
  251.8 7.1 %collective-permute-start.21 = (f32[4,16,1,64]{3,1,2,0:T(8,128)S(1)}, f32[4,16,1,64]{3,1,2,0:T(8,128)S(1)}, u32[]{:S(2)}, u32[]{:S(2)}) collective-permute-start(f32[4,16,1,64]{3,1,2,0:T(8,128)S(1)} %get-tuple-element.221), channel_id=1, source_target_pairs={{64,0},{128,64},{192,128},{256,192},{320,256},{384,320},{448,384},... | collective-permute-start | bytes 49160 | tf_op jit(solution)/shard_map/ppermute | solution.py:18
  259.8 11.1 %collective-permute-start.22 = (f32[4,16,10,1]{3,1,2,0:T(8,128)}, f32[4,16,10,1]{3,1,2,0:T(8,128)S(1)}, u32[]{:S(2)}, u32[]{:S(2)}) collective-permute-start(f32[4,16,10,1]{3,1,2,0:T(8,128)} %get-tuple-element.210), channel_id=1, source_target_pairs={{0,1},{1,2},{2,3},{3,4},{4,5},{5,6},{6,7},{7,8},{8,9},{9,10},{10,1... | collective-permute-start | bytes 7688 | tf_op jit(solution)/shard_map/ppermute | solution.py:15
  263.1 11.9 %collective-permute-start.23 = (f32[4,16,10,1]{3,1,2,0:T(8,128)S(1)}, f32[4,16,10,1]{3,1,2,0:T(8,128)S(1)}, u32[]{:S(2)}, u32[]{:S(2)}) collective-permute-start(f32[4,16,10,1]{3,1,2,0:T(8,128)S(1)} %get-tuple-element.211), channel_id=1, source_target_pairs={{1,0},{2,1},{3,2},{4,3},{5,4},{6,5},{7,6},{8,7},{9,8},{10,9},{11,1... | collective-permute-start | bytes 7688 | tf_op jit(solution)/shard_map/ppermute | solution.py:18
  275.7 6.9 %copy-start.15 = (f32[4,16,16,128]{3,1,2,0:T(8,128)S(1)}, f32[4,16,16,128]{3,1,2,0:T(8,128)}, u32[]{:S(2)}) copy-start(f32[4,16,16,128]{3,1,2,0:T(8,128)} %get-tuple-element.265) | copy-start | bytes 1572868
  279.7 11.2 %copy-start.2 = (f32[1,4,16,8,64]{4,2,0,3,1:T(8,128)S(1)}, f32[1,4,16,8,64]{4,2,0,3,1:T(8,128)}, u32[]{:S(2)}) copy-start(f32[1,4,16,8,64]{4,2,0,3,1:T(8,128)} %copy-done.1) | copy-start | bytes 393220
  279.7 11.2 %copy-start.4 = (f32[1,4,16,8,64]{4,2,0,3,1:T(8,128)S(1)}, f32[1,4,16,8,64]{4,2,0,3,1:T(8,128)}, u32[]{:S(2)}) copy-start(f32[1,4,16,8,64]{4,2,0,3,1:T(8,128)} %copy-done.3) | copy-start | bytes 393220
  282.6 28.4 %copy-start.6 = (f32[1,4,4,16,128]{4,2,0,3,1:T(4,128)S(1)}, f32[1,4,4,16,128]{4,2,0,3,1:T(4,128)}, u32[]{:S(2)}) copy-start(f32[1,4,4,16,128]{4,2,0,3,1:T(4,128)} %copy-done.5) | copy-start | bytes 393220
  282.6 28.4 %copy-start.8 = (f32[1,4,4,16,128]{4,2,0,3,1:T(4,128)S(1)}, f32[1,4,4,16,128]{4,2,0,3,1:T(4,128)}, u32[]{:S(2)}) copy-start(f32[1,4,4,16,128]{4,2,0,3,1:T(4,128)} %copy-done.7) | copy-start | bytes 393220
  283.5 8.3 %collective-permute-start.24 = (f32[4,4,1,128]{3,1,2,0:T(4,128)S(1)}, f32[4,4,1,128]{3,1,2,0:T(4,128)S(1)}, u32[]{:S(2)}, u32[]{:S(2)}) collective-permute-start(f32[4,4,1,128]{3,1,2,0:T(4,128)S(1)} %get-tuple-element.250), channel_id=1, source_target_pairs={{0,64},{64,128},{128,192},{192,256},{256,320},{320,384},{384,448},... | collective-permute-start | bytes 24584 | tf_op jit(solution)/shard_map/ppermute | solution.py:15
  285.4 6.4 %collective-permute-start.25 = (f32[4,4,1,128]{3,1,2,0:T(4,128)S(1)}, f32[4,4,1,128]{3,1,2,0:T(4,128)S(1)}, u32[]{:S(2)}, u32[]{:S(2)}) collective-permute-start(f32[4,4,1,128]{3,1,2,0:T(4,128)S(1)} %get-tuple-element.251), channel_id=1, source_target_pairs={{64,0},{128,64},{192,128},{256,192},{320,256},{384,320},{448,384},... | collective-permute-start | bytes 24584 | tf_op jit(solution)/shard_map/ppermute | solution.py:18
  292.1 6.6 %collective-permute-start.26 = (f32[4,4,18,1]{3,1,2,0:T(4,128)S(1)}, f32[4,4,18,1]{3,1,2,0:T(4,128)S(1)}, u32[]{:S(2)}, u32[]{:S(2)}) collective-permute-start(f32[4,4,18,1]{3,1,2,0:T(4,128)S(1)} %get-tuple-element.238), channel_id=1, source_target_pairs={{0,1},{1,2},{2,3},{3,4},{4,5},{5,6},{6,7},{7,8},{8,9},{9,10},{10,1... | collective-permute-start | bytes 3464 | tf_op jit(solution)/shard_map/ppermute | solution.py:15
  295.1 8.0 %collective-permute-start.27 = (f32[4,4,18,1]{3,1,2,0:T(4,128)S(1)}, f32[4,4,18,1]{3,1,2,0:T(4,128)S(1)}, u32[]{:S(2)}, u32[]{:S(2)}) collective-permute-start(f32[4,4,18,1]{3,1,2,0:T(4,128)S(1)} %get-tuple-element.239), channel_id=1, source_target_pairs={{1,0},{2,1},{3,2},{4,3},{5,4},{6,5},{7,6},{8,7},{9,8},{10,9},{11,1... | collective-permute-start | bytes 3464 | tf_op jit(solution)/shard_map/ppermute | solution.py:18
  303.3 112.9 %collective-permute-start.28 = (f32[4,4,1,128]{3,1,2,0:T(4,128)S(1)}, f32[4,4,1,128]{3,1,2,0:T(4,128)S(1)}, u32[]{:S(2)}, u32[]{:S(2)}) collective-permute-start(f32[4,4,1,128]{3,1,2,0:T(4,128)S(1)} %get-tuple-element.246), channel_id=1, source_target_pairs={{0,64},{64,128},{128,192},{192,256},{256,320},{320,384},{384,448},... | collective-permute-start | bytes 24584 | tf_op jit(solution)/shard_map/ppermute | solution.py:15
  305.2 110.9 %collective-permute-start.29 = (f32[4,4,1,128]{3,1,2,0:T(4,128)S(1)}, f32[4,4,1,128]{3,1,2,0:T(4,128)S(1)}, u32[]{:S(2)}, u32[]{:S(2)}) collective-permute-start(f32[4,4,1,128]{3,1,2,0:T(4,128)S(1)} %get-tuple-element.247), channel_id=1, source_target_pairs={{64,0},{128,64},{192,128},{256,192},{320,256},{384,320},{448,384},... | collective-permute-start | bytes 24584 | tf_op jit(solution)/shard_map/ppermute | solution.py:18
  416.4 7.7 %collective-permute-start.30 = (f32[4,4,18,1]{3,1,2,0:T(4,128)S(1)}, f32[4,4,18,1]{3,1,2,0:T(4,128)S(1)}, u32[]{:S(2)}, u32[]{:S(2)}) collective-permute-start(f32[4,4,18,1]{3,1,2,0:T(4,128)S(1)} %get-tuple-element.236), channel_id=1, source_target_pairs={{0,1},{1,2},{2,3},{3,4},{4,5},{5,6},{6,7},{7,8},{8,9},{9,10},{10,1... | collective-permute-start | bytes 3464 | tf_op jit(solution)/shard_map/ppermute | solution.py:15
  420.6 8.0 %collective-permute-start.31 = (f32[4,4,18,1]{3,1,2,0:T(4,128)S(1)}, f32[4,4,18,1]{3,1,2,0:T(4,128)S(1)}, u32[]{:S(2)}, u32[]{:S(2)}) collective-permute-start(f32[4,4,18,1]{3,1,2,0:T(4,128)S(1)} %get-tuple-element.237), channel_id=1, source_target_pairs={{1,0},{2,1},{3,2},{4,3},{5,4},{6,5},{7,6},{8,7},{9,8},{10,9},{11,1... | collective-permute-start | bytes 3464 | tf_op jit(solution)/shard_map/ppermute | solution.py:18
where the time goes:
time: 431 us; the launch traced here: 429 us
  blocking collectives  219 us (51%)
  starting transfers between devices  129 us (30%)
  waiting for transfers between devices  32.8 us (8%)
  other arithmetic  21.7 us (5%)
  local copies, waits for them, and re-layouts  17.1 us (4%)
  matrix products  8.29 us (2%)
    psum x1, blocking collectives, on_device(): features = lax.psum(act1.sum(axis=(2, 3)), ('face', 'tile')) / pooled_count  115 us
    psum x1, blocking collectives, on_device(): grad_f, grad_c = lax.psum((grad_f, grad_c), ('face', 'tile'))  104 us
    ppermute x16, starting transfers between devices, with_halo(): lax.ppermute(lax.slice_in_dim(block, 0, width, axis=dim), axis, backward)  82.5 us
    ppermute x16, starting transfers between devices, with_halo(): lax.ppermute(lax.slice_in_dim(block, block.shape[dim] - width, None, axis...  46.8 us
    ppermute x16, waiting for transfers between devices, with_halo(): lax.ppermute(lax.slice_in_dim(block, 0, width, axis=dim), axis, backward)  27.6 us
  transfers between devices with their start and end apart: 32, of which 13 were waited for; matrix products, arithmetic and copies ran while one was open for 4% of the time, Pallas kernels for 0%

commit v1 on v0

--- a/solution.py
+++ b/solution.py
@@ -99,7 +99,9 @@
     pre1 = jnp.einsum("kio,kbirc->borc", coarse_weight, terms1, precision=exact)
     act1 = jax.nn.softplus(pre1)
     pooled_count = nrows // 2 * lax.axis_size("face") * (ncols // 2) * lax.axis_size("tile")
-    features = lax.psum(act1.sum(axis=(2, 3)), ("face", "tile")) / pooled_count
+    features = (
+        jnp.sum(lax.all_gather(act1.sum(axis=(2, 3)), ("face", "tile")), axis=0) / pooled_count
+    )
     hidden = jnp.tanh(
         jnp.dot(features, feature_weight, precision=exact)
         + jnp.dot(params, param_weight, precision=exact)

time: 431 us -> 1010 us (2.34)
  blocking collectives: 219 us -> 795 us
    all_gather x0 -> x1, blocking collectives: none -> 691 us  [on_device(): lax.all_gather(act1.sum(axis=(2, 3)), ('face', 'tile'))]
    psum x1 -> x0, blocking collectives: 115 us -> none  [on_device(): features = lax.psum(act1.sum(axis=(2, 3)), ('face', 'tile')) / pooled_count]
  transfers between devices with their start and end apart: 32 -> 32, of which waited for: 13 -> 12; matrix products, arithmetic and copies ran while one was open for 4% -> 2% of each run, Pallas kernels for 0% -> 0%
where the time goes in v1:
time: 1010 us; the launch traced here: 1000 us
  blocking collectives  795 us (79%)
  starting transfers between devices  130 us (13%)
  waiting for transfers between devices  31.3 us (3%)
  other arithmetic  22.3 us (2%)
  local copies, waits for them, and re-layouts  16.4 us (2%)
    all_gather x1, blocking collectives, on_device(): lax.all_gather(act1.sum(axis=(2, 3)), ('face', 'tile'))  691 us
    psum x1, blocking collectives, on_device(): grad_f, grad_c = lax.psum((grad_f, grad_c), ('face', 'tile'))  104 us
    ppermute x16, starting transfers between devices, with_halo(): lax.ppermute(lax.slice_in_dim(block, 0, width, axis=dim), axis, backward)  82.9 us
    ppermute x16, starting transfers between devices, with_halo(): lax.ppermute(lax.slice_in_dim(block, block.shape[dim] - width, None, axis...  47.2 us
    ppermute x16, waiting for transfers between devices, with_halo(): lax.ppermute(lax.slice_in_dim(block, 0, width, axis=dim), axis, backward)  22.6 us
  transfers between devices with their start and end apart: 32, of which 12 were waited for; matrix products, arithmetic and copies ran while one was open for 2% of the time, Pallas kernels for 0%

profile of v1, /device:TPU:1, one launch (start us, length us, event | category | flops | bytes accessed | tf_op | source)
XLA Modules:
  0.0 1004.5 jit_solution(6925591644373757440)
XLA Ops:
  0.7 0.9 fusion.42
  1.6 4.0 collective-permute-start
  5.6 4.1 collective-permute-start.1
  9.8 0.8 fusion.58
  12.0 6.0 collective-permute-start.2
  18.1 4.5 collective-permute-start.3
  22.8 1.3 select_dynamic-update-slice_fusion.14
  24.2 1.9 collective-permute-done.3
  26.3 2.6 collective-permute-start.4
  28.9 4.8 collective-permute-start.5
  33.7 0.8 collective-permute-done.5
  34.7 2.9 collective-permute-start.6
  37.6 6.9 collective-permute-start.7
  44.7 0.7 select_dynamic-update-slice_fusion.12
  46.1 1.1 fusion.37
  47.2 1.7 compare_select_fusion.1
  49.0 2.6 copy.39
  51.6 5.6 reduce_sum.27
  57.6 2.5 collective-permute-start.8
  60.1 5.4 collective-permute-start.9
  65.6 1.0 collective-permute-done.9
  66.8 2.1 collective-permute-start.10
  68.8 9.0 collective-permute-start.11
  79.7 1.9 collective-permute-start.12
  81.6 6.2 collective-permute-start.13
  87.8 1.0 collective-permute-done.13
  89.1 2.1 collective-permute-start.14
  91.2 11.0 %collective-permute-start.15 = (f32[4,16,10,1]{3,1,2,0:T(8,128)S(1)}, f32[4,16,10,1]{3,1,2,0:T(8,128)S(1)}, u32[]{:S(2)}, u32[]{:S(2)}) collective-permute-start(f32[4,16,10,1]{3,1,2,0:T(8,128)S(1)} %get-tuple-element.215), channel_id=1, source_target_pairs={{1,0},{2,1},{3,2},{4,3},{5,4},{6,5},{7,6},{8,7},{9,8},{10,9},{11,1... | collective-permute-start | bytes 7688 | tf_op jit(solution)/shard_map/ppermute | solution.py:18
  104.1 1.0 fusion.1
  105.2 690.6 %all-gather.1 = f32[512,4,32]{2,1,0:T(4,128)S(1)} all-gather(f32[1,4,32]{2,1,0:T(4,128)S(1)} %bitcast.127), channel_id=2, replica_groups=mesh['face'=8,'tile'=64] {'face','tile'}, dimensions={0}, use_global_device_ids=true | all-gather | bytes 262656 | tf_op jit(solution)/shard_map/all_gather | solution.py:103
  797.6 0.9 convolution_bitcast_fusion
  798.6 1.9 collective-permute-start.16
  800.5 5.5 collective-permute-start.17
  806.0 1.0 collective-permute-done.17
  807.0 0.9 fusion.70
  807.9 5.0 collective-permute-start.18
  812.9 1.9 collective-permute-start.19
  816.4 4.3 collective-permute-done.18
  820.7 3.5 collective-permute-done.19
  824.5 1.9 collective-permute-start.20
  826.5 6.4 collective-permute-start.21
  832.9 1.0 collective-permute-done.21
  833.9 0.9 fusion.69
  834.8 3.2 collective-permute-start.22
  838.0 1.9 collective-permute-start.23
  841.5 4.3 collective-permute-done.22
  845.9 3.6 collective-permute-done.23
  850.1 4.0 broadcast_in_dim.2
  854.1 2.8 copy.45
  857.0 0.9 convolution_bitcast_fusion.3
  857.9 1.9 collective-permute-start.24
  859.8 5.7 collective-permute-start.25
  865.5 0.9 convolution_bitcast_fusion.4
  866.7 3.3 collective-permute-start.26
  869.9 1.9 collective-permute-start.27
  872.1 0.7 select_dynamic-update-slice_fusion.10
  873.5 4.4 collective-permute-done.27
  878.2 1.9 collective-permute-start.28
  880.1 5.7 collective-permute-start.29
  885.9 1.7 convolution_bitcast_fusion.5
  887.5 103.9 %all-reduce = (f32[3,4,16]{2,1,0:T(4,128)}, f32[3,16,32]{2,1,0:T(8,128)}) all-reduce(f32[3,4,16]{2,1,0:T(4,128)S(1)} %convolution_bitcast_fusion.5, f32[3,16,32]{2,1,0:T(8,128)S(1)} %convolution_bitcast_fusion.4), channel_id=1, replica_groups=mesh['face'=8,'tile'=64] {'face','tile'}, use_global_device_ids=true, to_apply=%region_3.4 | all-reduce | flops 1728 | bytes 13824 | tf_op jit(solution)/shard_map/psum | solution.py:127
  991.6 4.0 collective-permute-start.30
  995.6 1.9 collective-permute-start.31
  999.1 4.4 collective-permute-done.31
  (130 shorter events, 17.4 us)
Async XLA Ops:
  0.6 103.5 %copy-start = (f32[3,16,32]{2,1,0:T(8,128)S(1)}, f32[3,16,32]{2,1,0:T(8,128)}, u32[]{:S(2)}) copy-start(f32[3,16,32]{2,1,0:T(8,128)} %param.46) | copy-start | bytes 18436
  0.6 46.6 %copy-start.12 = (f32[3,4,16]{2,1,0:T(4,128)S(1)}, f32[3,4,16]{2,1,0:T(4,128)}, u32[]{:S(2)}) copy-start(f32[3,4,16]{2,1,0:T(4,128)} %param.45) | copy-start | bytes 2308
  1.6 50.0 %copy-start.7 = (f32[1,4,4,16,128]{4,2,0,3,1:T(4,128)}, f32[1,4,4,16,128]{4,2,0,3,1:T(4,128)S(1)}, u32[]{:S(2)}) copy-start(f32[1,4,4,16,128]{4,2,0,3,1:T(4,128)S(1)} %get-tuple-element.260) | copy-start | bytes 393220
  1.6 10.3 %collective-permute-start = (f32[4,4,1,128]{3,1,2,0:T(4,128)S(1)}, f32[4,4,1,128]{3,1,2,0:T(4,128)S(1)}, u32[]{:S(2)}, u32[]{:S(2)}) collective-permute-start(f32[4,4,1,128]{3,1,2,0:T(4,128)S(1)} %get-tuple-element.258), channel_id=1, source_target_pairs={{0,64},{64,128},{128,192},{192,256},{256,320},{320,384},{384,448},... | collective-permute-start | bytes 24584 | tf_op jit(solution)/shard_map/ppermute | solution.py:15
  5.6 6.2 collective-permute-start.1
  12.0 12.1 %collective-permute-start.2 = (f32[4,4,18,1]{3,1,2,0:T(4,128)S(1)}, f32[4,4,18,1]{3,1,2,0:T(4,128)S(1)}, u32[]{:S(2)}, u32[]{:S(2)}) collective-permute-start(f32[4,4,18,1]{3,1,2,0:T(4,128)S(1)} %get-tuple-element.242), channel_id=1, source_target_pairs={{0,1},{1,2},{2,3},{3,4},{4,5},{5,6},{6,7},{7,8},{8,9},{9,10},{10,1... | collective-permute-start | bytes 3464 | tf_op jit(solution)/shard_map/ppermute | solution.py:15
  18.1 8.0 collective-permute-start.3
  26.3 7.4 collective-permute-start.4
  28.9 5.6 collective-permute-start.5
  34.7 11.4 %collective-permute-start.6 = (f32[4,4,18,1]{3,1,2,0:T(4,128)S(1)}, f32[4,4,18,1]{3,1,2,0:T(4,128)S(1)}, u32[]{:S(2)}, u32[]{:S(2)}) collective-permute-start(f32[4,4,18,1]{3,1,2,0:T(4,128)S(1)} %get-tuple-element.240), channel_id=1, source_target_pairs={{0,1},{1,2},{2,3},{3,4},{4,5},{5,6},{6,7},{7,8},{8,9},{9,10},{10,1... | collective-permute-start | bytes 3464 | tf_op jit(solution)/shard_map/ppermute | solution.py:15
  37.6 8.5 collective-permute-start.7
  47.2 4.4 copy-start.5
  57.6 8.0 collective-permute-start.8
  60.1 6.4 collective-permute-start.9
  66.8 12.6 %collective-permute-start.10 = (f32[4,16,10,1]{3,1,2,0:T(8,128)S(1)}, f32[4,16,10,1]{3,1,2,0:T(8,128)S(1)}, u32[]{:S(2)}, u32[]{:S(2)}) collective-permute-start(f32[4,16,10,1]{3,1,2,0:T(8,128)S(1)} %get-tuple-element.216), channel_id=1, source_target_pairs={{0,1},{1,2},{2,3},{3,4},{4,5},{5,6},{6,7},{7,8},{8,9},{9,10},{10,1... | collective-permute-start | bytes 7688 | tf_op jit(solution)/shard_map/ppermute | solution.py:15
  68.8 10.6 %collective-permute-start.11 = (f32[4,16,10,1]{3,1,2,0:T(8,128)S(1)}, f32[4,16,10,1]{3,1,2,0:T(8,128)S(1)}, u32[]{:S(2)}, u32[]{:S(2)}) collective-permute-start(f32[4,16,10,1]{3,1,2,0:T(8,128)S(1)} %get-tuple-element.217), channel_id=1, source_target_pairs={{1,0},{2,1},{3,2},{4,3},{5,4},{6,5},{7,6},{8,7},{9,8},{10,9},{11,1... | collective-permute-start | bytes 7688 | tf_op jit(solution)/shard_map/ppermute | solution.py:18
  79.7 8.1 collective-permute-start.12
  81.6 7.2 collective-permute-start.13
  89.0 707.4 %copy-start.9 = (f32[32,128]{1,0:T(8,128)S(1)}, f32[32,128]{1,0:T(8,128)}, u32[]{:S(2)}) copy-start(f32[32,128]{1,0:T(8,128)} %param.47) | copy-start | bytes 49156
  89.0 707.5 %copy-start.10 = (f32[4,2]{0,1:T(2,128)S(1)}, f32[4,2]{0,1:T(2,128)}, u32[]{:S(2)}) copy-start(f32[4,2]{0,1:T(2,128)} %param.42) | copy-start | bytes 100
  89.0 707.5 %copy-start.11 = (f32[2,128]{1,0:T(2,128)S(1)}, f32[2,128]{1,0:T(2,128)}, u32[]{:S(2)}) copy-start(f32[2,128]{1,0:T(2,128)} %param.48) | copy-start | bytes 3076
  89.0 707.7 %copy-start.13 = (s32[4]{0:T(128)S(1)}, s32[4]{0:T(128)}, u32[]{:S(2)}) copy-start(s32[4]{0:T(128)} %param.43) | copy-start | bytes 52
  89.1 707.7 %copy-start.14 = (f32[128]{0:T(128)S(1)}, f32[128]{0:T(128)}, u32[]{:S(2)}) copy-start(f32[128]{0:T(128)} %param.49) | copy-start | bytes 1540
  89.1 14.7 %collective-permute-start.14 = (f32[4,16,10,1]{3,1,2,0:T(8,128)S(1)}, f32[4,16,10,1]{3,1,2,0:T(8,128)S(1)}, u32[]{:S(2)}, u32[]{:S(2)}) collective-permute-start(f32[4,16,10,1]{3,1,2,0:T(8,128)S(1)} %get-tuple-element.214), channel_id=1, source_target_pairs={{0,1},{1,2},{2,3},{3,4},{4,5},{5,6},{6,7},{7,8},{8,9},{9,10},{10,1... | collective-permute-start | bytes 7688 | tf_op jit(solution)/shard_map/ppermute | solution.py:15
  91.2 12.6 %collective-permute-start.15 = (f32[4,16,10,1]{3,1,2,0:T(8,128)S(1)}, f32[4,16,10,1]{3,1,2,0:T(8,128)S(1)}, u32[]{:S(2)}, u32[]{:S(2)}) collective-permute-start(f32[4,16,10,1]{3,1,2,0:T(8,128)S(1)} %get-tuple-element.215), channel_id=1, source_target_pairs={{1,0},{2,1},{3,2},{4,3},{5,4},{6,5},{7,6},{8,7},{9,8},{10,9},{11,1... | collective-permute-start | bytes 7688 | tf_op jit(solution)/shard_map/ppermute | solution.py:18
  104.1 1.1 copy-start.1
  104.1 1.1 copy-start.3
  798.6 7.4 collective-permute-start.16
  800.5 6.5 collective-permute-start.17
  807.9 12.8 %collective-permute-start.18 = (f32[4,16,10,1]{3,1,2,0:T(8,128)}, f32[4,16,10,1]{3,1,2,0:T(8,128)S(1)}, u32[]{:S(2)}, u32[]{:S(2)}) collective-permute-start(f32[4,16,10,1]{3,1,2,0:T(8,128)} %get-tuple-element.212), channel_id=1, source_target_pairs={{0,1},{1,2},{2,3},{3,4},{4,5},{5,6},{6,7},{7,8},{8,9},{9,10},{10,1... | collective-permute-start | bytes 7688 | tf_op jit(solution)/shard_map/ppermute | solution.py:15
  812.9 11.4 %collective-permute-start.19 = (f32[4,16,10,1]{3,1,2,0:T(8,128)S(1)}, f32[4,16,10,1]{3,1,2,0:T(8,128)S(1)}, u32[]{:S(2)}, u32[]{:S(2)}) collective-permute-start(f32[4,16,10,1]{3,1,2,0:T(8,128)S(1)} %get-tuple-element.213), channel_id=1, source_target_pairs={{1,0},{2,1},{3,2},{4,3},{5,4},{6,5},{7,6},{8,7},{9,8},{10,9},{11,1... | collective-permute-start | bytes 7688 | tf_op jit(solution)/shard_map/ppermute | solution.py:18
  824.5 8.3 collective-permute-start.20
  826.5 7.4 collective-permute-start.21
  834.8 11.1 %collective-permute-start.22 = (f32[4,16,10,1]{3,1,2,0:T(8,128)}, f32[4,16,10,1]{3,1,2,0:T(8,128)S(1)}, u32[]{:S(2)}, u32[]{:S(2)}) collective-permute-start(f32[4,16,10,1]{3,1,2,0:T(8,128)} %get-tuple-element.210), channel_id=1, source_target_pairs={{0,1},{1,2},{2,3},{3,4},{4,5},{5,6},{6,7},{7,8},{8,9},{9,10},{10,1... | collective-permute-start | bytes 7688 | tf_op jit(solution)/shard_map/ppermute | solution.py:15
  838.0 11.4 %collective-permute-start.23 = (f32[4,16,10,1]{3,1,2,0:T(8,128)S(1)}, f32[4,16,10,1]{3,1,2,0:T(8,128)S(1)}, u32[]{:S(2)}, u32[]{:S(2)}) collective-permute-start(f32[4,16,10,1]{3,1,2,0:T(8,128)S(1)} %get-tuple-element.211), channel_id=1, source_target_pairs={{1,0},{2,1},{3,2},{4,3},{5,4},{6,5},{7,6},{8,7},{9,8},{10,9},{11,1... | collective-permute-start | bytes 7688 | tf_op jit(solution)/shard_map/ppermute | solution.py:18
  850.1 6.9 copy-start.15
  854.1 11.4 %copy-start.2 = (f32[1,4,16,8,64]{4,2,0,3,1:T(8,128)S(1)}, f32[1,4,16,8,64]{4,2,0,3,1:T(8,128)}, u32[]{:S(2)}) copy-start(f32[1,4,16,8,64]{4,2,0,3,1:T(8,128)} %copy-done.1) | copy-start | bytes 393220
  854.1 11.4 %copy-start.4 = (f32[1,4,16,8,64]{4,2,0,3,1:T(8,128)S(1)}, f32[1,4,16,8,64]{4,2,0,3,1:T(8,128)}, u32[]{:S(2)}) copy-start(f32[1,4,16,8,64]{4,2,0,3,1:T(8,128)} %copy-done.3) | copy-start | bytes 393220
  857.0 28.9 %copy-start.6 = (f32[1,4,4,16,128]{4,2,0,3,1:T(4,128)S(1)}, f32[1,4,4,16,128]{4,2,0,3,1:T(4,128)}, u32[]{:S(2)}) copy-start(f32[1,4,4,16,128]{4,2,0,3,1:T(4,128)} %copy-done.5) | copy-start | bytes 393220
  857.0 28.9 %copy-start.8 = (f32[1,4,4,16,128]{4,2,0,3,1:T(4,128)S(1)}, f32[1,4,4,16,128]{4,2,0,3,1:T(4,128)}, u32[]{:S(2)}) copy-start(f32[1,4,4,16,128]{4,2,0,3,1:T(4,128)} %copy-done.7) | copy-start | bytes 393220
  857.9 8.6 collective-permute-start.24
  859.8 6.6 collective-permute-start.25
  866.7 6.8 collective-permute-start.26
  869.9 8.0 collective-permute-start.27
  878.2 113.2 %collective-permute-start.28 = (f32[4,4,1,128]{3,1,2,0:T(4,128)S(1)}, f32[4,4,1,128]{3,1,2,0:T(4,128)S(1)}, u32[]{:S(2)}, u32[]{:S(2)}) collective-permute-start(f32[4,4,1,128]{3,1,2,0:T(4,128)S(1)} %get-tuple-element.246), channel_id=1, source_target_pairs={{0,64},{64,128},{128,192},{192,256},{256,320},{320,384},{384,448},... | collective-permute-start | bytes 24584 | tf_op jit(solution)/shard_map/ppermute | solution.py:15
  880.1 111.3 %collective-permute-start.29 = (f32[4,4,1,128]{3,1,2,0:T(4,128)S(1)}, f32[4,4,1,128]{3,1,2,0:T(4,128)S(1)}, u32[]{:S(2)}, u32[]{:S(2)}) collective-permute-start(f32[4,4,1,128]{3,1,2,0:T(4,128)S(1)} %get-tuple-element.247), channel_id=1, source_target_pairs={{64,0},{128,64},{192,128},{256,192},{320,256},{384,320},{448,384},... | collective-permute-start | bytes 24584 | tf_op jit(solution)/shard_map/ppermute | solution.py:18
  991.6 7.5 collective-permute-start.30
  995.6 8.0 collective-permute-start.31
